TPU v7x, 32 devices: a whole 2x2x4 slice. The times are simulated.
32 devices in a mesh: dp: 4 (over y, core), ctx: 8 (over z, x).
Axes of the slice: x: 2, y: 2, z: 4, core: 2. Of those that a mesh axis runs over, the one named last changes fastest.
Arguments:
- queries: bfloat16 [4, 6144, 2048], P('dp', 'ctx'), may hold values from -6 to 6
- keys: bfloat16 [4, 6144, 2048], P('dp', 'ctx'), may hold values from -6 to 6
- values: bfloat16 [4, 6144, 2048], P('dp', 'ctx'), may hold values from -6 to 6
- grad_out: bfloat16 [4, 6144, 2048], P('dp', 'ctx'), may hold values from -6 to 6
- node_ids: int32 [4, 6144], P('dp', 'ctx'), may hold values from 0 to 383, never falling along the last dimension, each value on 1 to 64 neighbouring positions
- flags: int32 [4, 6144], P('dp', 'ctx'), may hold values 0 or 1
- gain: float32 [16], replicated, may hold values from 0.1 to 1.9
Outputs:
- grad_queries: bfloat16 [4, 6144, 2048], P('dp', 'ctx')
- grad_keys: bfloat16 [4, 6144, 2048], P('dp', 'ctx')
- grad_values: bfloat16 [4, 6144, 2048], P('dp', 'ctx')
- grad_gain: float32 [16], replicated
Inputs may be any that keep to these rules, and one draw needn't show every extreme that they name: `node_ids`: node numbers never fall along the tokens of a repository; a node spans 1 to 64 tokens.
All inputs are finite; a program needn't handle non-finite values. No bound on the sum of `flags` on one device may be relied on, other than what follows from the above.
Results may differ from a plain program's by a relative error of at most 0.0049.
Values sent between devices are 32-bit elements; how exact they have to be, the bound alone decides.
A program may use at most 128 MiB of HBM per device.

v0:
```python
import math

import jax
import jax.numpy as jnp
from jax import lax
from jax.sharding import PartitionSpec as P

H = 16
HD = 128
BLOCK = 128


def entering(part, axis, combine, identity, reverse):
    count = lax.axis_size(axis)
    place = lax.axis_index(axis)
    ahead = count - 1 - place if reverse else place
    gathered = lax.all_gather(part, axis)
    state = jnp.zeros_like(part) + jnp.asarray(identity, part.dtype)

    def one(step, state):
        source = count - 1 - step if reverse else step
        return combine(state, lax.dynamic_index_in_dim(gathered, source, 0, False))

    return lax.fori_loop(0, ahead, one, state)


def add_states(earlier, later):
    return earlier + later


def on_device(queries, keys, values, grad_out, node_ids, flags, gain):
    length = queries.shape[1]
    count = length // BLOCK
    scale = 1.0 / math.sqrt(HD * length * lax.axis_size("ctx"))
    q_blk = queries.reshape(count, BLOCK, H, HD)
    k_blk = keys.reshape(count, BLOCK, H, HD)
    v_blk = values.reshape(count, BLOCK, H, HD)
    g_blk = grad_out.reshape(count, BLOCK, H, HD)
    nodes = node_ids.reshape(count, BLOCK)
    marks = flags.reshape(count, BLOCK)
    rows = lax.broadcasted_iota(jnp.int32, (BLOCK, BLOCK), 0)
    cols = lax.broadcasted_iota(jnp.int32, (BLOCK, BLOCK), 1)
    causal = (cols <= rows)[None]
    linked = (nodes[:, :, None] == nodes[:, None, :]) | (marks[:, None, :] == 1)
    seen = (causal & linked).astype(jnp.float32)[:, None]
    kv_blk = jnp.einsum("bshd,bshe->bhde", k_blk, v_blk, preferred_element_type=jnp.float32)
    qg_blk = jnp.einsum("bthd,bthe->bhde", q_blk, g_blk, preferred_element_type=jnp.float32)
    own_kv = jnp.sum(kv_blk, axis=0)
    own_qg = jnp.sum(qg_blk, axis=0)
    carried = own_kv[None]
    before = entering(carried, "ctx", add_states, jnp.zeros_like(carried), False)
    prior_kv = before[0]
    scores = jnp.einsum("bthd,bshd->bhts", q_blk, k_blk, preferred_element_type=jnp.float32) * seen
    dscores = jnp.einsum("bthd,bshd->bhts", g_blk, v_blk, preferred_element_type=jnp.float32) * seen
    intra_term = jnp.sum(scores * dscores, axis=(0, 2, 3))
    pm = scores.astype(jnp.bfloat16)
    dpm = dscores.astype(jnp.bfloat16)
    dq_near = jnp.einsum("bhts,bshd->bthd", dpm, k_blk, preferred_element_type=jnp.float32)
    dk_near = jnp.einsum("bhts,bthd->bshd", dpm, q_blk, preferred_element_type=jnp.float32)
    dv_near = jnp.einsum("bhts,bthd->bshd", pm, g_blk, preferred_element_type=jnp.float32)
    later_qg = entering(own_qg[None], "ctx", add_states, jnp.zeros_like(own_qg[None]), True)[0]
    zero = jnp.zeros((1,) + kv_blk.shape[1:], jnp.float32)
    prior = prior_kv[None] + jnp.cumsum(jnp.concatenate([zero, kv_blk[:-1]], axis=0), axis=0)
    later = later_qg[None] + jnp.flip(
        jnp.cumsum(jnp.flip(jnp.concatenate([qg_blk[1:], zero], axis=0), 0), axis=0), 0
    )
    inter_term = jnp.sum(prior * qg_blk, axis=(0, 2, 3))
    prior_h = prior.astype(jnp.bfloat16)
    later_h = later.astype(jnp.bfloat16)
    factor = (scale * gain)[None, None, :, None]
    dq = dq_near + jnp.einsum("bthe,bhde->bthd", g_blk, prior_h, preferred_element_type=jnp.float32)
    dk = dk_near + jnp.einsum("bshe,bhde->bshd", v_blk, later_h, preferred_element_type=jnp.float32)
    dv = dv_near + jnp.einsum("bshd,bhde->bshe", k_blk, later_h, preferred_element_type=jnp.float32)
    shape = queries.shape
    grad_queries = (dq * factor).astype(jnp.bfloat16).reshape(shape)
    grad_keys = (dk * factor).astype(jnp.bfloat16).reshape(shape)
    grad_values = (dv * factor).astype(jnp.bfloat16).reshape(shape)
    term = scale * (intra_term + inter_term)
    total = lax.psum(term, ("dp", "ctx"))
    norm_tokens = lax.axis_size("dp") * length * lax.axis_size("ctx") * HD
    grad_gain = (total / math.sqrt(norm_tokens)).astype(jnp.float32)
    return (grad_queries, grad_keys, grad_values, grad_gain)


def solution(mesh):
    placed = (
        P("dp", "ctx", None),
        P("dp", "ctx", None),
        P("dp", "ctx", None),
        P("dp", "ctx", None),
        P("dp", "ctx"),
        P("dp", "ctx"),
        P(),
    )
    return jax.shard_map(
        on_device,
        mesh=mesh,
        in_specs=placed,
        out_specs=(P("dp", "ctx", None), P("dp", "ctx", None), P("dp", "ctx", None), P()),
        check_vma=False,
    )
```

profile of v0, /device:TPU:0, one launch (start us, length us, event | category | flops | bytes accessed | tf_op | source)
XLA Modules:
  0.0 347.5 jit_solution(15812434154692063138)
XLA Ops:
  7.2 0.0 all-gather.5.cloned.1.call-start
  7.2 3.0 copy.87
  10.3 1.0 copy.86
  11.3 0.7 copy-done.2
  12.0 5.4 %fusion.31 = (f32[16,128,128]{2,1,0:T(8,128)}, f32[6,16,128,128]{3,2,1,0:T(8,128)}) fusion(bf16[6,128,16,128]{3,2,1,0:T(8,128)(2,1)S(1)} %bitcast.80, bf16[6,128,16,128]{3,2,1,0:T(8,128)(2,1)S(1)} %bitcast.73), kind=kOutput, calls=%fused_computation.48 | convolution fusion | flops 403963904 | bytes 13631488 | tf_op jit(solution)/shard_map/bshd,bshe->bhde/dot_general | solution.py:46
  17.4 0.0 all-gather.5.cloned.1.call-update
  17.4 0.0 all-gather.7.cloned.1.call-start
  17.5 3.0 copy.85
  20.6 2.7 copy.88
  23.3 2.4 copy-done.11
  25.6 3.5 %fusion.6 = f32[6,16,128,128]{3,2,1,0:T(8,128)} fusion(f32[6,16,128,128]{3,2,1,0:T(8,128)S(1)} %copy-done.11), kind=kOutput, calls=%fused_computation.17 | output fusion | flops 7864320 | bytes 11534336 | tf_op jit(solution)/shard_map/jit(cumsum)/reduce_window_sum | solution.py:63
  29.1 116.1 %all-gather.5.cloned.1.call-done = f32[128,128,128]{2,1,0:T(8,128)} async-done(((f32[16,128,128]{2,1,0:T(8,128)}), f32[128,128,128]{2,1,0:T(8,128)}) %all-gather.5.cloned.1.call-update) | async-done | bytes 8388624 | tf_op jit(solution)/shard_map/all_gather | solution.py:17
  145.2 1.1 broadcast.36.clone
  146.3 9.9 %multiply_reduce_fusion = (f32[16]{0:T(128)S(1)}, f32[16,128,128]{2,1,0:T(8,128)}, f32[6,16,128,128]{3,2,1,0:T(8,128)}) fusion(f32[6,16,128,128]{3,2,1,0:T(8,128)} %fusion.6, f32[16,128,128]{2,1,0:T(8,128)} %bitcast.77, bf16[6,128,16,128]{3,2,1,0:T(8,128)(2,1)S(1)} %bitcast.69, bf16[6,128,16,128]{3,2,1,0:T(8,128)(2,1)} %bitcast.83), kind=kOutput, calls=%fused_computation.11 | convolution fusion | flops 408682496 | bytes 20971584 | tf_op jit(solution)/shard_map/bthd,bthe->bhde/dot_general | solution.py:47
  156.2 0.0 all-gather.7.cloned.1.call-update
  156.4 0.2 and_convert_fusion
  156.6 4.3 %fusion.21 = f32[6,16,128,128]{3,2,1,0:T(8,128)S(1)} fusion(bf16[6,128,16,128]{3,2,1,0:T(8,128)(2,1)} %bitcast.81, bf16[6,128,16,128]{3,2,1,0:T(8,128)(2,1)S(1)} %bitcast.70), kind=kOutput, calls=%fused_computation.32 | convolution fusion | flops 402653184 | bytes 12582912 | tf_op jit(solution)/shard_map/bthd,bshd->bhts/dot_general | solution.py:54
  160.9 4.2 %fusion.16 = f32[6,16,128,128]{3,2,1,0:T(8,128)} fusion(bf16[6,128,16,128]{3,2,1,0:T(8,128)(2,1)S(1)} %bitcast.84, f32[6,16,128,128]{3,2,1,0:T(8,128)S(1)} %fusion.21, f32[6,128,128]{2,1,0:T(8,128)S(1)} %and_convert_fusion), kind=kOutput, calls=%fused_computation.27 | convolution fusion | flops 405798912 | bytes 16121856 | tf_op jit(solution)/shard_map/bhts,bthd->bshd/dot_general | solution.py:59
  165.2 0.9 copy-done
  166.1 3.2 multiply_reduce_fusion.1
  169.2 4.2 %fusion.9 = f32[6,16,128,128]{3,2,1,0:T(8,128)} fusion(f32[6,16,128,128]{3,2,1,0:T(8,128)S(1)} %get-tuple-element.115, f32[6,128,128]{2,1,0:T(8,128)S(1)} %and_convert_fusion, bf16[6,128,16,128]{3,2,1,0:T(8,128)(2,1)S(1)} %bitcast.71), kind=kOutput, calls=%fused_computation.20 | convolution fusion | flops 405798912 | bytes 16121856 | tf_op jit(solution)/shard_map/bhts,bthd->bshd/dot_general | solution.py:60
  173.4 57.7 %psum.7 = f32[16]{0:T(128)S(1)} all-reduce(f32[16]{0:T(128)S(1)} %add_multiply_fusion), channel_id=1, replica_groups=mesh['dp'=4,'ctx'=8] {'dp','ctx'}, use_global_device_ids=true, to_apply=%region_10.11 | all-reduce | flops 16 | bytes 128 | tf_op jit(solution)/shard_map/psum | solution.py:79
  231.1 2.9 slice.9
  234.0 3.3 concatenate.4
  237.3 6.3 %rev.7 = f32[6,16,128,128]{3,2,1,0:T(8,128)} reverse(f32[6,16,128,128]{3,2,1,0:T(8,128)} %concatenate.4), dimensions={0} | reverse | bytes 12582912 | tf_op jit(solution)/shard_map/jit(_flip)/rev | solution.py:65
  243.6 6.1 %fusion.8 = f32[6,16,128,128]{2,3,1,0:T(8,128)S(1)} fusion(f32[6,16,128,128]{3,2,1,0:T(8,128)} %fusion.6, f32[16,128,128]{2,1,0:T(8,128)S(1)} %bitcast.78, bf16[6,128,16,128]{3,2,1,0:T(8,128)(2,1)} %bitcast.72), kind=kOutput, calls=%fused_computation.19 | convolution fusion | flops 405798912 | bytes 16777216 | tf_op jit(solution)/shard_map/bthe,bhde->bthd/dot_general | solution.py:71
  249.8 3.7 %fusion.5 = bf16[6,128,16,128]{3,1,2,0:T(8,128)(2,1)} fusion(f32[6,16,128,128]{2,3,1,0:T(8,128)S(1)} %fusion.8, f32[16]{0:T(128)S(1)} %broadcast_multiply_fusion.1, bf16[6,128,16,128]{3,2,1,0:T(8,128)(2,1)S(1)} %bitcast.75, f32[6,16,128,128]{3,2,1,0:T(8,128)S(1)} %bitcast.68, f32[6,128,128]{2,1,0:T(8,128)S(1)} %and_convert_fusion), kind=kOutput, calls=%fused_computation.10 | convolution fusion | flops 410517504 | bytes 19267648 | tf_op jit(solution)/shard_map/bhts,bshd->bthd/dot_general | solution.py:58
  253.5 3.9 %copy.62 = bf16[6,128,16,128]{3,2,1,0:T(8,128)(2,1)S(1)} copy(bf16[6,128,16,128]{3,1,2,0:T(8,128)(2,1)} %fusion.5) | data formatting | bytes 6291456 | tf_op jit(solution)/shard_map/convert_element_type | solution.py:75
  257.4 3.3 reshape.55
  260.7 0.5 broadcast_multiply_fusion
  261.2 6.5 %fusion.32 = f32[6,16,128,128]{3,2,1,0:T(8,128)} fusion(f32[6,16,128,128]{3,2,1,0:T(8,128)} %rev.7), kind=kOutput, calls=%fused_computation.49 | output fusion | flops 7864320 | bytes 12582912 | tf_op jit(solution)/shard_map/jit(cumsum)/reduce_window_sum | solution.py:65
  267.8 31.6 %all-gather.7.cloned.1.call-done = f32[128,128,128]{2,1,0:T(8,128)} async-done(((f32[16,128,128]{2,1,0:T(8,128)}), f32[128,128,128]{2,1,0:T(8,128)}) %all-gather.7.cloned.1.call-update) | async-done | bytes 8388624 | tf_op jit(solution)/shard_map/all_gather | solution.py:17
  299.4 0.1 broadcast.36
  299.5 10.9 %while.23 = (s32[]{:T(128)}, f32[1,16,128,128]{3,2,1,0:T(8,128)S(1)}, s32[]{:T(128)}, f32[8,1,16,128,128]{4,3,2,1,0:T(8,128)}, s32[]{:T(128)}, /*index=5*/s32[]{:T(128)}, s32[]{:T(128)}, s32[]{:T(128)}) while((s32[]{:T(128)}, f32[1,16,128,128]{3,2,1,0:T(8,128)S(1)}, s32[]{:T(128)}, f32[8,1,16,128,128]{4,3,2,1,0:T(8,128)}, s32[]{:T(128)}, ...), condition=%wide.region_6.7_spmd, body=%wide.region_5.6_spmd.sunk | while | flops 262150 | bytes 3145863 | solution.py:24
  299.5 1.5 bitcast_add_fusion.8
  301.0 1.5 bitcast_add_fusion.8
  302.5 1.5 bitcast_add_fusion.8
  304.1 1.5 bitcast_add_fusion.8
  305.6 1.5 bitcast_add_fusion.8
  307.1 1.5 bitcast_add_fusion.8
  308.6 1.5 bitcast_add_fusion.8
  310.4 3.8 %add_convert_fusion = bf16[6,16,128,128]{3,2,1,0:T(8,128)(2,1)S(1)} fusion(f32[6,16,128,128]{3,2,1,0:T(8,128)} %fusion.32, f32[16,128,128]{2,1,0:T(8,128)S(1)} %bitcast.79), kind=kLoop, calls=%fused_computation.13 | loop fusion | flops 3145728 | bytes 10485760 | tf_op jit(solution)/shard_map/convert_element_type | solution.py:69
  314.2 5.4 %fusion.1 = bf16[6,128,16,128]{3,1,2,0:T(8,128)(2,1)S(1)} fusion(f32[6,16,128,128]{3,2,1,0:T(8,128)} %fusion.9, f32[16]{0:T(128)S(1)} %broadcast_multiply_fusion.1, bf16[6,16,128,128]{3,2,1,0:T(8,128)(2,1)S(1)} %add_convert_fusion, bf16[6,128,16,128]{3,2,1,0:T(8,128)(2,1)S(1)} %bitcast.76), kind=kOutput, calls=%fused_computation.4 | convolution fusion | flops 407371776 | bytes 15728704 | tf_op jit(solution)/shard_map/bshd,bhde->bshe/dot_general | solution.py:73
  319.6 3.7 %copy.78 = bf16[6,128,16,128]{3,2,1,0:T(8,128)(2,1)} copy(bf16[6,128,16,128]{3,1,2,0:T(8,128)(2,1)S(1)} %fusion.1) | data formatting | bytes 6291456 | tf_op jit(solution)/shard_map/convert_element_type | solution.py:77
  323.3 5.9 %reshape.58 = bf16[1,768,2048]{2,1,0:T(8,128)(2,1)} reshape(bf16[6,128,16,128]{3,2,1,0:T(8,128)(2,1)} %copy.78) | data formatting | bytes 6291456 | tf_op jit(solution)/shard_map/reshape | solution.py:77
  329.2 6.0 %fusion.3 = bf16[6,128,16,128]{3,1,2,0:T(8,128)(2,1)S(1)} fusion(f32[6,16,128,128]{3,2,1,0:T(8,128)} %fusion.16, f32[16]{0:T(128)S(1)} %broadcast_multiply_fusion.1, bf16[6,16,128,128]{3,2,1,0:T(8,128)(2,1)} %copy-done.10, bf16[6,128,16,128]{3,2,1,0:T(8,128)(2,1)S(1)} %bitcast.82), kind=kOutput, calls=%fused_computation.7 | convolution fusion | flops 407371776 | bytes 15728704 | tf_op jit(solution)/shard_map/bshe,bhde->bshd/dot_general | solution.py:72
  335.3 2.0 copy.70
  337.3 3.3 reshape.57
  (42 shorter events, 0.1 us)
Async XLA Ops:
  7.2 138.1 %all-gather.5.cloned.1.call-start = ((), (), s32[]{:S(2)}) async-start(), calls=%async_computation | async-start | bytes 9437184 | tf_op jit(solution)/shard_map/all_gather | solution.py:17
  7.2 3.1 copy-start.12
  10.3 1.8 copy-start.2
  11.3 6.1 %copy-start.7 = (bf16[96,8,16,128]{3,2,1,0:T(8,128)(2,1)}, bf16[96,8,16,128]{3,2,1,0:T(8,128)(2,1)S(1)}, u32[]{:S(2)}) copy-start(bf16[96,8,16,128]{3,2,1,0:T(8,128)(2,1)S(1)} %copy.86) | copy-start | bytes 9437188
  17.4 281.9 %all-gather.7.cloned.1.call-start = ((), (), s32[]{:S(2)}) async-start(), calls=%async_computation.1 | async-start | bytes 9437184 | tf_op jit(solution)/shard_map/all_gather | solution.py:17
  17.5 3.1 copy-start.13
  20.6 148.7 %copy-start.1 = (bf16[96,8,16,128]{3,2,1,0:T(8,128)(2,1)}, bf16[96,8,16,128]{3,2,1,0:T(8,128)(2,1)S(1)}, u32[]{:S(2)}) copy-start(bf16[96,8,16,128]{3,2,1,0:T(8,128)(2,1)S(1)} %copy.85) | copy-start | bytes 9437188
  20.6 5.1 %copy-start.11 = (f32[6,16,128,128]{3,2,1,0:T(8,128)S(1)}, f32[6,16,128,128]{3,2,1,0:T(8,128)}, u32[]{:S(2)}) copy-start(f32[6,16,128,128]{3,2,1,0:T(8,128)} %get-tuple-element.112) | copy-start | bytes 18874372
  146.3 10.0 %copy-start.15 = (s32[1,768]{1,0:T(1,128)S(1)}, s32[1,768]{1,0:T(1,128)}, u32[]{:S(2)}) copy-start(s32[1,768]{1,0:T(1,128)} %param.15) | copy-start | bytes 9220
  146.3 10.0 %copy-start.14 = (s32[1,768]{1,0:T(1,128)S(1)}, s32[1,768]{1,0:T(1,128)}, u32[]{:S(2)}) copy-start(s32[1,768]{1,0:T(1,128)} %param.16) | copy-start | bytes 9220
  146.3 10.1 %copy-start.16 = (f32[16]{0:T(128)S(1)}, f32[16]{0:T(128)}, u32[]{:S(2)}) copy-start(f32[16]{0:T(128)} %param.17) | copy-start | bytes 196
  156.6 4.4 %copy-start.9 = (bf16[96,8,16,128]{3,2,1,0:T(8,128)(2,1)S(1)}, bf16[96,8,16,128]{3,2,1,0:T(8,128)(2,1)}, u32[]{:S(2)}) copy-start(bf16[96,8,16,128]{3,2,1,0:T(8,128)(2,1)} %copy.88) | copy-start | bytes 9437188
  160.9 5.1 %copy-start = (f32[6,16,128,128]{3,2,1,0:T(8,128)}, f32[6,16,128,128]{3,2,1,0:T(8,128)S(1)}, u32[]{:S(2)}) copy-start(f32[6,16,128,128]{3,2,1,0:T(8,128)S(1)} %fusion.21) | copy-start | bytes 18874372
  160.9 5.1 %copy-start.3 = (bf16[96,8,16,128]{3,2,1,0:T(8,128)(2,1)S(1)}, bf16[96,8,16,128]{3,2,1,0:T(8,128)(2,1)}, u32[]{:S(2)}) copy-start(bf16[96,8,16,128]{3,2,1,0:T(8,128)(2,1)} %copy-done.2) | copy-start | bytes 9437188
  237.3 6.3 %copy-start.6 = (f32[1,16,128,128]{3,2,1,0:T(8,128)S(1)}, f32[1,16,128,128]{3,2,1,0:T(8,128)}, u32[]{:S(2)}) copy-start(f32[1,16,128,128]{3,2,1,0:T(8,128)} %get-tuple-element.83) | copy-start | bytes 3145732
  237.3 12.5 %slice-start = ((s8[6291456]{0:T(1024)(128)(4,1)}), s8[2097152]{0:T(1024)(128)(4,1)S(1)}, s32[]{:S(2)}) async-start(s8[6291456]{0:T(1024)(128)(4,1)} %bitcast.67), calls=%async_computation.2 | async-start | bytes 4194304
  243.6 6.2 %slice-start.1 = ((s8[6291456]{0:T(1024)(128)(4,1)}), s8[4194304]{0:T(1024)(128)(4,1)S(1)}, s32[]{:S(2)}) async-start(s8[6291456]{0:T(1024)(128)(4,1)} %bitcast.67), calls=%async_computation.3 | async-start | bytes 8388608
  243.6 6.2 %copy-start.4 = (bf16[96,8,16,128]{3,2,1,0:T(8,128)(2,1)S(1)}, bf16[96,8,16,128]{3,2,1,0:T(8,128)(2,1)}, u32[]{:S(2)}) copy-start(bf16[96,8,16,128]{3,2,1,0:T(8,128)(2,1)} %copy-done.2) | copy-start | bytes 9437188
  310.4 3.8 %copy-start.5 = (bf16[96,8,16,128]{3,2,1,0:T(8,128)(2,1)S(1)}, bf16[96,8,16,128]{3,2,1,0:T(8,128)(2,1)}, u32[]{:S(2)}) copy-start(bf16[96,8,16,128]{3,2,1,0:T(8,128)(2,1)} %copy-done.2) | copy-start | bytes 9437188
  314.2 5.4 %copy-start.10 = (bf16[6,16,128,128]{3,2,1,0:T(8,128)(2,1)}, bf16[6,16,128,128]{3,2,1,0:T(8,128)(2,1)S(1)}, u32[]{:S(2)}) copy-start(bf16[6,16,128,128]{3,2,1,0:T(8,128)(2,1)S(1)} %add_convert_fusion) | copy-start | bytes 9437188
  323.3 5.9 %copy-start.8 = (bf16[96,8,16,128]{3,2,1,0:T(8,128)(2,1)S(1)}, bf16[96,8,16,128]{3,2,1,0:T(8,128)(2,1)}, u32[]{:S(2)}) copy-start(bf16[96,8,16,128]{3,2,1,0:T(8,128)(2,1)} %copy-done.7) | copy-start | bytes 9437188
Sparse Core Ops, SparseCore 0:
  17.6 127.6 all-gather.4
  156.4 142.9 all-gather.6
where the time goes:
time: 348 us; the launch traced here: 347 us
  waiting for transfers between devices  148 us (43%)
  blocking collectives  57.7 us (17%)
  matrix products  52.5 us (15%)
  local copies, waits for them, and re-layouts  49.6 us (14%)
  other arithmetic  25 us (7%)
  between operations  14.4 us (4%)
    all_gather x2, waiting for transfers between devices, entering(): gathered = lax.all_gather(part, axis)  148 us
    psum x1, blocking collectives, on_device(): total = lax.psum(term, ('dp', 'ctx'))  57.7 us
    unnamed x42, local copies, waits for them, and re-layouts  13.8 us
    add x7, other arithmetic, add_states(): return earlier + later  10.4 us
    dot_general x1, matrix products, on_device(): jnp.einsum('bthd,bthe->bhde', q_blk, g_blk, preferred_element_type=jnp.fl...  9.94 us
  transfers between devices with their start and end apart: 2, of which 2 were waited for; matrix products, arithmetic and copies ran while one was open for 18% of the time, Pallas kernels for 0%

commit v1 on v0

v1 whole, which is shorter than its diff:
```python
import math

import jax
import jax.numpy as jnp
from jax import lax
from jax.experimental import pallas as pl
from jax.experimental.pallas import tpu as pltpu
from jax.sharding import PartitionSpec as P

H = 16
HD = 128
BLOCK = 128
PER = 2
CHUNKS = 2


def nt(a, b):
    return lax.dot_general(a, b, (((1,), (1,)), ((), ())), preferred_element_type=jnp.float32)


def tn(a, b):
    return lax.dot_general(a, b, (((0,), (0,)), ((), ())), preferred_element_type=jnp.float32)


def nn(a, b):
    return lax.dot_general(a, b, (((1,), (0,)), ((), ())), preferred_element_type=jnp.float32)


def cols(i):
    return slice(i * HD, (i + 1) * HD)


def state_kernel(q_ref, k_ref, v_ref, g_ref, kv_ref, qg_ref):
    for i in range(PER):
        kv_ref[i] = tn(k_ref[0, :, cols(i)], v_ref[0, :, cols(i)])
        qg_ref[i] = tn(q_ref[0, :, cols(i)], g_ref[0, :, cols(i)])


def term_kernel(q_ref, k_ref, v_ref, g_ref, seen_ref, term_ref):
    count = q_ref.shape[1] // BLOCK
    for i in range(PER):
        total = jnp.zeros((BLOCK, HD), jnp.float32)
        state = jnp.zeros((HD, HD), jnp.float32)
        for b in range(count):
            at = (0, slice(b * BLOCK, (b + 1) * BLOCK), cols(i))
            q, k, v, g = q_ref[at], k_ref[at], v_ref[at], g_ref[at]
            total = total + nt(q, k) * nt(g, v) * seen_ref[b]
            if b > 0:
                total = total + state * tn(q, g)
            if b < count - 1:
                state = state + tn(k, v)
        term_ref[i] = jnp.sum(total, axis=0, keepdims=True)


def grad_kernel(q_ref, k_ref, v_ref, g_ref, seen_ref, prior_ref, later_ref, factor_ref,
                dq_ref, dk_ref, dv_ref):
    count = q_ref.shape[1] // BLOCK
    step = pl.program_id(0)
    for i in range(PER):
        factor = factor_ref[step * PER + i]
        later = [later_ref[i]]
        for b in range(count - 1, 0, -1):
            at = (0, slice(b * BLOCK, (b + 1) * BLOCK), cols(i))
            later.append(later[-1] + tn(q_ref[at], g_ref[at]))
        later = [r.astype(jnp.bfloat16) for r in later[::-1]]
        prior = prior_ref[i]
        for b in range(count):
            at = (0, slice(b * BLOCK, (b + 1) * BLOCK), cols(i))
            q, k, v, g = q_ref[at], k_ref[at], v_ref[at], g_ref[at]
            seen = seen_ref[b]
            pm = (nt(q, k) * seen).astype(jnp.bfloat16)
            dpm = (nt(g, v) * seen).astype(jnp.bfloat16)
            s = prior.astype(jnp.bfloat16)
            r = later[b]
            dq_ref[at] = ((nn(dpm, k) + nt(g, s)) * factor).astype(jnp.bfloat16)
            dk_ref[at] = ((tn(dpm, q) + nt(v, r)) * factor).astype(jnp.bfloat16)
            dv_ref[at] = ((tn(pm, g) + nn(k, r)) * factor).astype(jnp.bfloat16)
            if b < count - 1:
                prior = prior + tn(k, v)


def cost(heads, length, products, extra):
    return pl.CostEstimate(
        flops=2 * heads * length * HD * HD * products,
        bytes_accessed=8 * heads * length * HD + extra,
        transcendentals=0,
    )


PARAMS = pltpu.CompilerParams(vmem_limit_bytes=40 * 1024 * 1024)


def on_device(queries, keys, values, grad_out, node_ids, flags, gain):
    length = queries.shape[1]
    count = length // BLOCK
    n = lax.axis_size("ctx")
    place = lax.axis_index("ctx")
    scale = 1.0 / math.sqrt(HD * length * n)
    tokens = (queries, keys, values, grad_out)

    def wide(first):
        return pl.BlockSpec((1, length, PER * HD), lambda i: (0, 0, i + first))

    state_spec = pl.BlockSpec((PER, HD, HD), lambda i: (i, 0, 0))
    group = H // CHUNKS
    states = []
    for c in range(CHUNKS):
        states.append(pl.pallas_call(
            state_kernel,
            grid=(group // PER,),
            in_specs=[wide(c * group // PER)] * 4,
            out_specs=[state_spec] * 2,
            out_shape=[jax.ShapeDtypeStruct((group, HD, HD), jnp.float32)] * 2,
            compiler_params=PARAMS,
            cost_estimate=cost(group, length, 2, 8 * group * HD * HD),
            name="states",
        )(*tokens))

    side = 2 if n % 2 == 0 else 1
    odd = (place % side) == 1
    swap = [(i, i ^ 1) for i in range(n)]
    up = [(i, i + side) for i in range(n - side)]
    down = [(i + side, i) for i in range(n - side)]
    priors, laters = [], []
    for kv, qg in states:
        if side == 2:
            kv_other = lax.ppermute(kv, "ctx", swap)
            qg_other = lax.ppermute(qg, "ctx", swap)
            prior = jnp.where(odd, kv_other, 0.0)
            later = jnp.where(odd, 0.0, qg_other)
            kv_move, qg_move = kv + kv_other, qg + qg_other
        else:
            prior, later = jnp.zeros_like(kv), jnp.zeros_like(qg)
            kv_move, qg_move = kv, qg
        for _ in range(n // side - 1):
            kv_move = lax.ppermute(kv_move, "ctx", up)
            qg_move = lax.ppermute(qg_move, "ctx", down)
            prior = prior + kv_move
            later = later + qg_move
        priors.append(prior)
        laters.append(later)

    nodes = node_ids.reshape(count, BLOCK)
    marks = flags.reshape(count, BLOCK)
    row = lax.broadcasted_iota(jnp.int32, (BLOCK, BLOCK), 0)
    col = lax.broadcasted_iota(jnp.int32, (BLOCK, BLOCK), 1)
    linked = (nodes[:, :, None] == nodes[:, None, :]) | (marks[:, None, :] == 1)
    seen = ((col <= row)[None] & linked).astype(jnp.float32)
    seen_spec = pl.BlockSpec((count, BLOCK, BLOCK), lambda i: (0, 0, 0))

    near = pl.pallas_call(
        term_kernel,
        grid=(H // PER,),
        in_specs=[wide(0)] * 4 + [seen_spec],
        out_specs=pl.BlockSpec((PER, 1, HD), lambda i: (i, 0, 0)),
        out_shape=jax.ShapeDtypeStruct((H, 1, HD), jnp.float32),
        compiler_params=PARAMS,
        cost_estimate=cost(H, length, 8, 0),
        name="gain_term",
    )(*tokens, seen)

    far = jnp.concatenate([
        jnp.sum(prior * qg, axis=(1, 2)) for prior, (_, qg) in zip(priors, states)
    ])
    term = scale * (jnp.sum(near, axis=(1, 2)) + far)
    total = lax.psum(term, ("dp", "ctx"))

    wide_out = jax.ShapeDtypeStruct(queries.shape, jnp.bfloat16)
    grads = pl.pallas_call(
        grad_kernel,
        grid=(H // PER,),
        in_specs=[wide(0)] * 4 + [seen_spec, state_spec, state_spec,
                                  pl.BlockSpec(memory_space=pltpu.SMEM)],
        out_specs=[wide(0)] * 3,
        out_shape=[wide_out] * 3,
        compiler_params=PARAMS,
        cost_estimate=cost(H, length, 20, 6 * H * length * HD),
        name="grads",
    )(*tokens, seen, jnp.concatenate(priors), jnp.concatenate(laters), scale * gain)

    norm_tokens = lax.axis_size("dp") * length * n * HD
    grad_gain = (total / math.sqrt(norm_tokens)).astype(jnp.float32)
    return (*grads, grad_gain)


def solution(mesh):
    rows = P("dp", "ctx", None)
    return jax.shard_map(
        on_device,
        mesh=mesh,
        in_specs=(rows, rows, rows, rows, P("dp", "ctx"), P("dp", "ctx"), P()),
        out_specs=(rows, rows, rows, P()),
        check_vma=False,
    )
```

time: 348 us -> 217 us (0.62)
  waiting for transfers between devices: 148 us -> 65.5 us
  matrix products: 52.5 us -> 0 us
  Pallas kernels: 0 us -> 41 us
  starting transfers between devices: 0.08 us -> 40.2 us
  local copies, waits for them, and re-layouts: 49.6 us -> 13.3 us
  blocking collectives: 57.7 us -> 42.2 us
  between operations: 14.4 us -> 0.88 us
  other arithmetic: 25 us -> 13.3 us
    all_gather x2 -> x0, waiting for transfers between devices: 148 us -> none  [entering(): gathered = lax.all_gather(part, axis)]
    ppermute x0 -> x16, waiting for transfers between devices: none -> 65.5 us  [the longest x6 31.1 us: on_device(): kv_move = lax.ppermute(kv_move, 'ctx', up)]
    dot_general x10 -> x0, matrix products: 52.5 us -> none  [the longest x1 9.94 us: on_device(): jnp.einsum('bthd,bthe->bhde', q_blk, g_blk, preferred_element_type=jnp.fl...]
    pallas_call x0 -> x4, Pallas kernels: none -> 41 us  [the longest x1 27 us: on_device(): pl.pallas_call(grad_kernel, grid=(H // PER,), in_specs=[wide(0)] * 4 + [s...]
    ppermute x0 -> x16, starting transfers between devices: none -> 40.2 us  [the longest x6 26.2 us: on_device(): kv_move = lax.ppermute(kv_move, 'ctx', up)]
    psum x1, blocking collectives: 57.7 us -> 42.2 us  [on_device(): total = lax.psum(term, ('dp', 'ctx'))]
    reshape x3 -> x0, local copies, waits for them, and re-layouts: 12.5 us -> none  [the longest x1 5.92 us: on_device(): grad_values = (dv * factor).astype(jnp.bfloat16).reshape(shape)]
    another operation x2 -> x0, other arithmetic: 10.1 us -> none  [the longest x1 6.55 us: on_device(): jnp.cumsum(jnp.flip(jnp.concatenate([qg_blk[1:], zero], axis=0), 0), axis=0)]
  transfers between devices with their start and end apart: 2 -> 16, of which waited for: 2 -> 10; matrix products, arithmetic and copies ran while one was open for 18% -> 5% of each run, Pallas kernels for 0% -> 5%
where the time goes in v1:
time: 217 us; the launch traced here: 216 us
  waiting for transfers between devices  65.5 us (30%)
  blocking collectives  42.2 us (19%)
  Pallas kernels  41 us (19%)
  starting transfers between devices  40.2 us (19%)
  local copies, waits for them, and re-layouts  13.3 us (6%)
  other arithmetic  13.3 us (6%)
    psum x1, blocking collectives, on_device(): total = lax.psum(term, ('dp', 'ctx'))  42.2 us
    ppermute x6, waiting for transfers between devices, on_device(): kv_move = lax.ppermute(kv_move, 'ctx', up)  31.1 us
    pallas_call x1, Pallas kernels, on_device(): pl.pallas_call(grad_kernel, grid=(H // PER,), in_specs=[wide(0)] * 4 + [s...  27 us
    ppermute x6, starting transfers between devices, on_device(): kv_move = lax.ppermute(kv_move, 'ctx', up)  26.2 us
    ppermute x6, waiting for transfers between devices, on_device(): qg_move = lax.ppermute(qg_move, 'ctx', down)  18.7 us
    ppermute x2, waiting for transfers between devices, on_device(): kv_other = lax.ppermute(kv, 'ctx', swap)  15.7 us
    unnamed x36, local copies, waits for them, and re-layouts  13.3 us
    pallas_call x1, Pallas kernels, on_device(): pl.pallas_call(term_kernel, grid=(H // PER,), in_specs=[wide(0)] * 4 + [s...  8.11 us
  transfers between devices with their start and end apart: 16, of which 10 were waited for; matrix products, arithmetic and copies ran while one was open for 5% of the time, Pallas kernels for 5%

profile of v1, /device:TPU:0, one launch (start us, length us, event | category | flops | bytes accessed | tf_op | source)
XLA Modules:
  0.0 216.4 jit_solution(12806089708334455420)
XLA Ops:
  0.6 1.9 copy-done
  2.5 1.9 copy-done.2
  4.4 1.9 copy-done.5
  6.3 1.9 copy-done.8
  8.2 2.6 %states.3 = (f32[8,128,128]{2,1,0:T(8,128)S(1)}, f32[8,128,128]{2,1,0:T(8,128)S(1)}) custom-call(bf16[1,768,2048]{2,1,0:T(8,128)(2,1)S(1)} %copy-done, bf16[1,768,2048]{2,1,0:T(8,128)(2,1)S(1)} %copy-done.2, bf16[1,768,2048]{2,1,0:T(8,128)(2,1)S(1)} %copy-done.5, bf16[1,768,2048]{2,1,0:T(8,128)(2,1)S(1)} %copy-done.8), custom_call_target="tpu_custom_call" | custom-call | flops 402653184 | bytes 7340032 | tf_op jit(solution)/shard_map/states/pallas_call | solution.py:108
  10.8 3.0 %collective-permute-start.4 = (f32[8,128,128]{2,1,0:T(8,128)S(1)}, f32[8,128,128]{2,1,0:T(8,128)S(1)}, u32[]{:S(2)}, u32[]{:S(2)}) collective-permute-start(f32[8,128,128]{2,1,0:T(8,128)S(1)} %get-tuple-element.12), channel_id=1, source_target_pairs={{0,1},{1,0},{2,3},{3,2},{4,5},{5,4},{6,7},{7,6},{8,9},{9,8},{10,11... | collective-permute-start | bytes 1572872 | tf_op jit(solution)/shard_map/ppermute | solution.py:127
  13.8 3.3 %states.2 = (f32[8,128,128]{2,1,0:T(8,128)S(1)}, f32[8,128,128]{2,1,0:T(8,128)}) custom-call(bf16[1,768,2048]{2,1,0:T(8,128)(2,1)S(1)} %copy-done, bf16[1,768,2048]{2,1,0:T(8,128)(2,1)S(1)} %copy-done.2, bf16[1,768,2048]{2,1,0:T(8,128)(2,1)S(1)} %copy-done.5, bf16[1,768,2048]{2,1,0:T(8,128)(2,1)S(1)} %copy-done.8), custom_call_target="tpu_custom_call" | custom-call | flops 402653184 | bytes 7340032 | tf_op jit(solution)/shard_map/states/pallas_call | solution.py:108
  17.1 9.5 %collective-permute-done.4 = f32[8,128,128]{2,1,0:T(8,128)S(1)} collective-permute-done((f32[8,128,128]{2,1,0:T(8,128)S(1)}, f32[8,128,128]{2,1,0:T(8,128)S(1)}, u32[]{:S(2)}, u32[]{:S(2)}) %collective-permute-start.4) | collective-permute-done | bytes 524320 | tf_op jit(solution)/shard_map/ppermute | solution.py:127
  26.6 4.1 %collective-permute-start.5 = (f32[8,128,128]{2,1,0:T(8,128)S(1)}, f32[8,128,128]{2,1,0:T(8,128)S(1)}, u32[]{:S(2)}, u32[]{:S(2)}) collective-permute-start(f32[8,128,128]{2,1,0:T(8,128)S(1)} %add.62), channel_id=1, source_target_pairs={{0,2},{1,3},{2,4},{3,5},{4,6},{5,7},{8,10},{9,11},{10,12},{11,13},... | collective-permute-start | bytes 1572872 | tf_op jit(solution)/shard_map/ppermute | solution.py:136
  30.7 6.3 %collective-permute-done = f32[8,128,128]{2,1,0:T(8,128)S(1)} collective-permute-done((f32[8,128,128]{2,1,0:T(8,128)S(1)}, f32[8,128,128]{2,1,0:T(8,128)S(1)}, u32[]{:S(2)}, u32[]{:S(2)}) %collective-permute-start) | collective-permute-done | bytes 524320 | tf_op jit(solution)/shard_map/ppermute | solution.py:127
  37.1 3.8 %collective-permute-start.1 = (f32[8,128,128]{2,1,0:T(8,128)S(1)}, f32[8,128,128]{2,1,0:T(8,128)S(1)}, u32[]{:S(2)}, u32[]{:S(2)}) collective-permute-start(f32[8,128,128]{2,1,0:T(8,128)S(1)} %add.58), channel_id=1, source_target_pairs={{0,2},{1,3},{2,4},{3,5},{4,6},{5,7},{8,10},{9,11},{10,12},{11,13},... | collective-permute-start | bytes 1572872 | tf_op jit(solution)/shard_map/ppermute | solution.py:136
  40.8 3.5 %collective-permute-start.6 = (f32[8,128,128]{2,1,0:T(8,128)S(1)}, f32[8,128,128]{2,1,0:T(8,128)S(1)}, u32[]{:S(2)}, u32[]{:S(2)}) collective-permute-start(f32[8,128,128]{2,1,0:T(8,128)S(1)} %collective-permute-done.5), channel_id=1, source_target_pairs={{0,2},{1,3},{2,4},{3,5},{4,6},{5,7},{8,10},{9,11},{10,12},{11,13},... | collective-permute-start | bytes 1572872 | tf_op jit(solution)/shard_map/ppermute | solution.py:136
  44.3 8.8 %collective-permute-done.1 = f32[8,128,128]{2,1,0:T(8,128)S(1)} collective-permute-done((f32[8,128,128]{2,1,0:T(8,128)S(1)}, f32[8,128,128]{2,1,0:T(8,128)S(1)}, u32[]{:S(2)}, u32[]{:S(2)}) %collective-permute-start.1) | collective-permute-done | bytes 524320 | tf_op jit(solution)/shard_map/ppermute | solution.py:136
  53.2 5.2 %collective-permute-start.2 = (f32[8,128,128]{2,1,0:T(8,128)S(1)}, f32[8,128,128]{2,1,0:T(8,128)}, u32[]{:S(2)}, u32[]{:S(2)}) collective-permute-start(f32[8,128,128]{2,1,0:T(8,128)S(1)} %collective-permute-done.1), channel_id=1, source_target_pairs={{0,2},{1,3},{2,4},{3,5},{4,6},{5,7},{8,10},{9,11},{10,12},{11,13},... | collective-permute-start | bytes 1572872 | tf_op jit(solution)/shard_map/ppermute | solution.py:136
  58.4 1.5 collective-permute-start.12
  59.9 4.5 %collective-permute-done.6 = f32[8,128,128]{2,1,0:T(8,128)S(1)} collective-permute-done((f32[8,128,128]{2,1,0:T(8,128)S(1)}, f32[8,128,128]{2,1,0:T(8,128)S(1)}, u32[]{:S(2)}, u32[]{:S(2)}) %collective-permute-start.6) | collective-permute-done | bytes 524320 | tf_op jit(solution)/shard_map/ppermute | solution.py:136
  64.4 4.4 %collective-permute-start.7 = (f32[8,128,128]{2,1,0:T(8,128)S(1)}, f32[8,128,128]{2,1,0:T(8,128)S(1)}, u32[]{:S(2)}, u32[]{:S(2)}) collective-permute-start(f32[8,128,128]{2,1,0:T(8,128)S(1)} %collective-permute-done.6), channel_id=1, source_target_pairs={{0,2},{1,3},{2,4},{3,5},{4,6},{5,7},{8,10},{9,11},{10,12},{11,13},... | collective-permute-start | bytes 1572872 | tf_op jit(solution)/shard_map/ppermute | solution.py:136
  68.8 1.6 collective-permute-start.8
  70.4 5.3 %collective-permute-done.2 = f32[8,128,128]{2,1,0:T(8,128)} collective-permute-done((f32[8,128,128]{2,1,0:T(8,128)S(1)}, f32[8,128,128]{2,1,0:T(8,128)}, u32[]{:S(2)}, u32[]{:S(2)}) %collective-permute-start.2) | collective-permute-done | bytes 524320 | tf_op jit(solution)/shard_map/ppermute | solution.py:136
  75.6 5.3 %collective-permute-start.3 = (f32[8,128,128]{2,1,0:T(8,128)}, f32[8,128,128]{2,1,0:T(8,128)}, u32[]{:S(2)}, u32[]{:S(2)}) collective-permute-start(f32[8,128,128]{2,1,0:T(8,128)} %collective-permute-done.2), channel_id=1, source_target_pairs={{0,2},{1,3},{2,4},{3,5},{4,6},{5,7},{8,10},{9,11},{10,12},{11,13},... | collective-permute-start | bytes 1572872 | tf_op jit(solution)/shard_map/ppermute | solution.py:136
  80.9 5.9 %collective-permute-done.7 = f32[8,128,128]{2,1,0:T(8,128)S(1)} collective-permute-done((f32[8,128,128]{2,1,0:T(8,128)S(1)}, f32[8,128,128]{2,1,0:T(8,128)S(1)}, u32[]{:S(2)}, u32[]{:S(2)}) %collective-permute-start.7) | collective-permute-done | bytes 524320 | tf_op jit(solution)/shard_map/ppermute | solution.py:136
  86.9 1.1 multiply_reduce_fusion
  88.0 1.6 collective-permute-start.13
  89.6 6.6 %collective-permute-done.3 = f32[8,128,128]{2,1,0:T(8,128)} collective-permute-done((f32[8,128,128]{2,1,0:T(8,128)}, f32[8,128,128]{2,1,0:T(8,128)}, u32[]{:S(2)}, u32[]{:S(2)}) %collective-permute-start.3) | collective-permute-done | bytes 524320 | tf_op jit(solution)/shard_map/ppermute | solution.py:136
  96.1 2.7 %multiply_reduce_fusion.1 = (f32[8]{0:T(128)S(1)}, f32[8,128,128]{2,1,0:T(8,128)}, f32[8,128,128]{2,1,0:T(8,128)}) fusion(f32[8,128,128]{2,1,0:T(8,128)} %get-tuple-element.13, f32[8,128,128]{2,1,0:T(8,128)} %collective-permute-done.3, f32[8,128,128]{2,1,0:T(8,128)} %collective-permute-done.2, f32[8,128,128]{2,1,0:T(8,128)S(1)} %copy-done.15, ...), kind=kLoop, calls=%fused_computation.3 | loop fusion | flops 917496 | bytes 4194337 | tf_op jit(solution)/shard_map/reduce_sum | solution.py:163
  98.8 1.3 collective-permute-start.9
  100.2 0.2 and_convert_fusion.seen_ref
  100.4 0.7 collective-permute-done.13
  101.0 1.3 collective-permute-start.14
  102.3 14.0 %collective-permute-done.9 = f32[8,128,128]{2,1,0:T(8,128)} collective-permute-done((f32[8,128,128]{2,1,0:T(8,128)}, f32[8,128,128]{2,1,0:T(8,128)}, u32[]{:S(2)}, u32[]{:S(2)}) %collective-permute-start.9) | collective-permute-done | bytes 524320 | tf_op jit(solution)/shard_map/ppermute | solution.py:137
  116.3 1.3 collective-permute-start.10
  117.7 1.9 copy-done.3
  119.5 1.9 copy-done.6
  121.4 1.9 copy-done.9
  123.3 8.1 %gain_term.1 = f32[16,1,128]{2,1,0:T(1,128)S(1)} custom-call(bf16[1,768,2048]{2,1,0:T(8,128)(2,1)S(1)} %copy-done.1, bf16[1,768,2048]{2,1,0:T(8,128)(2,1)S(1)} %copy-done.3, bf16[1,768,2048]{2,1,0:T(8,128)(2,1)S(1)} %copy-done.6, bf16[1,768,2048]{2,1,0:T(8,128)(2,1)S(1)} %copy-done.9, f32[6,128,128]{2,1,0:T(8,128)S(1)} %and_convert_fusion.seen_ref), custom_call_target="tpu_custom_call" | custom-call | flops 3221225472 | bytes 12582912 | tf_op jit(solution)/shard_map/gain_term/pallas_call | solution.py:151
  131.4 0.7 reduce_sum.27
  132.2 0.7 broadcast_multiply_fusion.1.factor_ref
  132.8 1.3 collective-permute-start.15
  134.1 0.7 fusion
  134.8 4.0 %collective-permute-done.10 = f32[8,128,128]{2,1,0:T(8,128)} collective-permute-done((f32[8,128,128]{2,1,0:T(8,128)}, f32[8,128,128]{2,1,0:T(8,128)}, u32[]{:S(2)}, u32[]{:S(2)}) %collective-permute-start.10) | collective-permute-done | bytes 524320 | tf_op jit(solution)/shard_map/ppermute | solution.py:137
  138.8 1.3 collective-permute-start.11
  140.1 2.3 %pad_maximum_fusion.prior_ref = f32[16,128,128]{2,1,0:T(8,128)} fusion(f32[8,128,128]{2,1,0:T(8,128)} %get-tuple-element.21, f32[8,128,128]{2,1,0:T(8,128)} %get-tuple-element.19), kind=kLoop, calls=%fused_computation | loop fusion | flops 262144 | bytes 2097152 | tf_op jit(solution)/shard_map/concatenate | solution.py:179
  142.4 42.2 %psum.7 = f32[16]{0:T(128)S(1)} all-reduce(f32[16]{0:T(128)S(1)} %fusion), channel_id=1, replica_groups=mesh['dp'=4,'ctx'=8] {'dp','ctx'}, use_global_device_ids=true, to_apply=%region_3.4 | all-reduce | flops 16 | bytes 128 | tf_op jit(solution)/shard_map/psum | solution.py:166
  184.6 0.5 broadcast_multiply_fusion
  185.1 1.8 add_add_fusion
  186.9 2.4 %add_add_fusion.1 = f32[8,128,128]{2,1,0:T(8,128)S(1)} fusion(f32[8,128,128]{2,1,0:T(8,128)} %collective-permute-done.11, f32[8,128,128]{2,1,0:T(8,128)} %collective-permute-done.10, f32[8,128,128]{2,1,0:T(8,128)} %collective-permute-done.9, f32[8,128,128]{2,1,0:T(8,128)} %collective-permute-done.8, pred[]{:T(512)S(6)} %eq.41), kind=kLoop, calls=%fused_computation.5 | loop fusion | flops 524288 | bytes 2621441 | tf_op jit(solution)/shard_map/add | solution.py:139
  189.3 0.1 pad_maximum_fusion.1.later_ref
  189.4 27.0 %grads.1 = (bf16[1,768,2048]{2,1,0:T(8,128)(2,1)}, bf16[1,768,2048]{2,1,0:T(8,128)(2,1)}, bf16[1,768,2048]{2,1,0:T(8,128)(2,1)}) custom-call(bf16[1,768,2048]{2,1,0:T(8,128)(2,1)S(1)} %copy-done.1, bf16[1,768,2048]{2,1,0:T(8,128)(2,1)S(1)} %copy-done.4, bf16[1,768,2048]{2,1,0:T(8,128)(2,1)S(1)} %copy-done.7, bf16[1,768,2048]{2,1,0:T(8,128)(2,1)} %g_ref.7, ...), custom_call_target="tpu_custom_call" | custom-call | flops 8053063680 | bytes 22020096 | tf_op jit(solution)/shard_map/grads/pallas_call | solution.py:169
  (41 shorter events, 0.3 us)
Async XLA Ops:
  0.6 1.9 copy-start
  2.5 1.9 copy-start.2
  4.4 1.9 copy-start.5
  6.3 1.9 copy-start.8
  10.8 15.8 %collective-permute-start.4 = (f32[8,128,128]{2,1,0:T(8,128)S(1)}, f32[8,128,128]{2,1,0:T(8,128)S(1)}, u32[]{:S(2)}, u32[]{:S(2)}) collective-permute-start(f32[8,128,128]{2,1,0:T(8,128)S(1)} %get-tuple-element.12), channel_id=1, source_target_pairs={{0,1},{1,0},{2,3},{3,2},{4,5},{5,4},{6,7},{7,6},{8,9},{9,8},{10,11... | collective-permute-start | bytes 1572872 | tf_op jit(solution)/shard_map/ppermute | solution.py:127
  17.1 19.9 %collective-permute-start = (f32[8,128,128]{2,1,0:T(8,128)S(1)}, f32[8,128,128]{2,1,0:T(8,128)S(1)}, u32[]{:S(2)}, u32[]{:S(2)}) collective-permute-start(f32[8,128,128]{2,1,0:T(8,128)S(1)} %get-tuple-element.11), channel_id=1, source_target_pairs={{0,1},{1,0},{2,3},{3,2},{4,5},{5,4},{6,7},{7,6},{8,9},{9,8},{10,11... | collective-permute-start | bytes 1572872 | tf_op jit(solution)/shard_map/ppermute | solution.py:127
  26.6 14.2 %collective-permute-start.5 = (f32[8,128,128]{2,1,0:T(8,128)S(1)}, f32[8,128,128]{2,1,0:T(8,128)S(1)}, u32[]{:S(2)}, u32[]{:S(2)}) collective-permute-start(f32[8,128,128]{2,1,0:T(8,128)S(1)} %add.62), channel_id=1, source_target_pairs={{0,2},{1,3},{2,4},{3,5},{4,6},{5,7},{8,10},{9,11},{10,12},{11,13},... | collective-permute-start | bytes 1572872 | tf_op jit(solution)/shard_map/ppermute | solution.py:136
  37.0 21.4 %copy-start.11 = (f32[8,128,128]{2,1,0:T(8,128)}, f32[8,128,128]{2,1,0:T(8,128)S(1)}, u32[]{:S(2)}) copy-start(f32[8,128,128]{2,1,0:T(8,128)S(1)} %collective-permute-done) | copy-start | bytes 1572868
  37.1 16.1 %collective-permute-start.1 = (f32[8,128,128]{2,1,0:T(8,128)S(1)}, f32[8,128,128]{2,1,0:T(8,128)S(1)}, u32[]{:S(2)}, u32[]{:S(2)}) collective-permute-start(f32[8,128,128]{2,1,0:T(8,128)S(1)} %add.58), channel_id=1, source_target_pairs={{0,2},{1,3},{2,4},{3,5},{4,6},{5,7},{8,10},{9,11},{10,12},{11,13},... | collective-permute-start | bytes 1572872 | tf_op jit(solution)/shard_map/ppermute | solution.py:136
  40.8 23.6 %collective-permute-start.6 = (f32[8,128,128]{2,1,0:T(8,128)S(1)}, f32[8,128,128]{2,1,0:T(8,128)S(1)}, u32[]{:S(2)}, u32[]{:S(2)}) collective-permute-start(f32[8,128,128]{2,1,0:T(8,128)S(1)} %collective-permute-done.5), channel_id=1, source_target_pairs={{0,2},{1,3},{2,4},{3,5},{4,6},{5,7},{8,10},{9,11},{10,12},{11,13},... | collective-permute-start | bytes 1572872 | tf_op jit(solution)/shard_map/ppermute | solution.py:136
  53.2 5.2 %copy-start.14 = (f32[8,128,128]{2,1,0:T(8,128)}, f32[8,128,128]{2,1,0:T(8,128)S(1)}, u32[]{:S(2)}) copy-start(f32[8,128,128]{2,1,0:T(8,128)S(1)} %collective-permute-done.1) | copy-start | bytes 1572868
  53.2 22.5 %collective-permute-start.2 = (f32[8,128,128]{2,1,0:T(8,128)S(1)}, f32[8,128,128]{2,1,0:T(8,128)}, u32[]{:S(2)}, u32[]{:S(2)}) collective-permute-start(f32[8,128,128]{2,1,0:T(8,128)S(1)} %collective-permute-done.1), channel_id=1, source_target_pairs={{0,2},{1,3},{2,4},{3,5},{4,6},{5,7},{8,10},{9,11},{10,12},{11,13},... | collective-permute-start | bytes 1572872 | tf_op jit(solution)/shard_map/ppermute | solution.py:136
  58.4 22.5 %collective-permute-start.12 = (f32[8,128,128]{2,1,0:T(8,128)S(1)}, f32[8,128,128]{2,1,0:T(8,128)S(1)}, u32[]{:S(2)}, u32[]{:S(2)}) collective-permute-start(f32[8,128,128]{2,1,0:T(8,128)S(1)} %get-tuple-element.14), channel_id=1, source_target_pairs={{0,1},{1,0},{2,3},{3,2},{4,5},{5,4},{6,7},{7,6},{8,9},{9,8},{10,11... | collective-permute-start | bytes 1572872 | tf_op jit(solution)/shard_map/ppermute | solution.py:128
  64.4 22.5 %collective-permute-start.7 = (f32[8,128,128]{2,1,0:T(8,128)S(1)}, f32[8,128,128]{2,1,0:T(8,128)S(1)}, u32[]{:S(2)}, u32[]{:S(2)}) collective-permute-start(f32[8,128,128]{2,1,0:T(8,128)S(1)} %collective-permute-done.6), channel_id=1, source_target_pairs={{0,2},{1,3},{2,4},{3,5},{4,6},{5,7},{8,10},{9,11},{10,12},{11,13},... | collective-permute-start | bytes 1572872 | tf_op jit(solution)/shard_map/ppermute | solution.py:136
  68.8 20.8 %collective-permute-start.8 = (f32[8,128,128]{2,1,0:T(8,128)}, f32[8,128,128]{2,1,0:T(8,128)}, u32[]{:S(2)}, u32[]{:S(2)}) collective-permute-start(f32[8,128,128]{2,1,0:T(8,128)} %get-tuple-element.13), channel_id=1, source_target_pairs={{0,1},{1,0},{2,3},{3,2},{4,5},{5,4},{6,7},{7,6},{8,9},{9,8},{10,11... | collective-permute-start | bytes 1572872 | tf_op jit(solution)/shard_map/ppermute | solution.py:128
  75.6 20.5 %collective-permute-start.3 = (f32[8,128,128]{2,1,0:T(8,128)}, f32[8,128,128]{2,1,0:T(8,128)}, u32[]{:S(2)}, u32[]{:S(2)}) collective-permute-start(f32[8,128,128]{2,1,0:T(8,128)} %collective-permute-done.2), channel_id=1, source_target_pairs={{0,2},{1,3},{2,4},{3,5},{4,6},{5,7},{8,10},{9,11},{10,12},{11,13},... | collective-permute-start | bytes 1572872 | tf_op jit(solution)/shard_map/ppermute | solution.py:136
  80.9 15.2 %copy-start.12 = (f32[8,128,128]{2,1,0:T(8,128)S(1)}, f32[8,128,128]{2,1,0:T(8,128)}, u32[]{:S(2)}) copy-start(f32[8,128,128]{2,1,0:T(8,128)} %copy-done.11) | copy-start | bytes 1572868
  80.9 15.2 %copy-start.15 = (f32[8,128,128]{2,1,0:T(8,128)S(1)}, f32[8,128,128]{2,1,0:T(8,128)}, u32[]{:S(2)}) copy-start(f32[8,128,128]{2,1,0:T(8,128)} %copy-done.14) | copy-start | bytes 1572868
  80.9 6.0 %copy-start.13 = (f32[8,128,128]{2,1,0:T(8,128)}, f32[8,128,128]{2,1,0:T(8,128)S(1)}, u32[]{:S(2)}) copy-start(f32[8,128,128]{2,1,0:T(8,128)S(1)} %collective-permute-done.12) | copy-start | bytes 1572868
  88.0 12.1 %copy-start.17 = (s32[1,768]{1,0:T(1,128)S(1)}, s32[1,768]{1,0:T(1,128)}, u32[]{:S(2)}) copy-start(s32[1,768]{1,0:T(1,128)} %param.11) | copy-start | bytes 9220
  88.0 12.1 %copy-start.16 = (s32[1,768]{1,0:T(1,128)S(1)}, s32[1,768]{1,0:T(1,128)}, u32[]{:S(2)}) copy-start(s32[1,768]{1,0:T(1,128)} %param.12) | copy-start | bytes 9220
  88.0 29.6 %copy-start.1 = (bf16[1,768,2048]{2,1,0:T(8,128)(2,1)S(1)}, bf16[1,768,2048]{2,1,0:T(8,128)(2,1)}, u32[]{:S(2)}) copy-start(bf16[1,768,2048]{2,1,0:T(8,128)(2,1)} %q_ref.7) | copy-start | bytes 9437188
  88.0 13.0 %collective-permute-start.13 = (f32[8,128,128]{2,1,0:T(8,128)}, f32[8,128,128]{2,1,0:T(8,128)}, u32[]{:S(2)}, u32[]{:S(2)}) collective-permute-start(f32[8,128,128]{2,1,0:T(8,128)} %get-tuple-element.23), channel_id=1, source_target_pairs={{2,0},{3,1},{4,2},{5,3},{6,4},{7,5},{10,8},{11,9},{12,10},{13,11},... | collective-permute-start | bytes 1572872 | tf_op jit(solution)/shard_map/ppermute | solution.py:137
  98.8 17.5 %collective-permute-start.9 = (f32[8,128,128]{2,1,0:T(8,128)}, f32[8,128,128]{2,1,0:T(8,128)}, u32[]{:S(2)}, u32[]{:S(2)}) collective-permute-start(f32[8,128,128]{2,1,0:T(8,128)} %get-tuple-element.22), channel_id=1, source_target_pairs={{2,0},{3,1},{4,2},{5,3},{6,4},{7,5},{10,8},{11,9},{12,10},{13,11},... | collective-permute-start | bytes 1572872 | tf_op jit(solution)/shard_map/ppermute | solution.py:137
  101.0 31.8 %collective-permute-start.14 = (f32[8,128,128]{2,1,0:T(8,128)}, f32[8,128,128]{2,1,0:T(8,128)}, u32[]{:S(2)}, u32[]{:S(2)}) collective-permute-start(f32[8,128,128]{2,1,0:T(8,128)} %collective-permute-done.13), channel_id=1, source_target_pairs={{2,0},{3,1},{4,2},{5,3},{6,4},{7,5},{10,8},{11,9},{12,10},{13,11},... | collective-permute-start | bytes 1572872 | tf_op jit(solution)/shard_map/ppermute | solution.py:137
  116.3 22.5 %collective-permute-start.10 = (f32[8,128,128]{2,1,0:T(8,128)}, f32[8,128,128]{2,1,0:T(8,128)}, u32[]{:S(2)}, u32[]{:S(2)}) collective-permute-start(f32[8,128,128]{2,1,0:T(8,128)} %collective-permute-done.9), channel_id=1, source_target_pairs={{2,0},{3,1},{4,2},{5,3},{6,4},{7,5},{10,8},{11,9},{12,10},{13,11},... | collective-permute-start | bytes 1572872 | tf_op jit(solution)/shard_map/ppermute | solution.py:137
  117.6 1.9 copy-start.3
  119.5 1.9 copy-start.6
  121.4 1.9 copy-start.9
  132.8 52.3 %collective-permute-start.15 = (f32[8,128,128]{2,1,0:T(8,128)}, f32[8,128,128]{2,1,0:T(8,128)}, u32[]{:S(2)}, u32[]{:S(2)}) collective-permute-start(f32[8,128,128]{2,1,0:T(8,128)} %collective-permute-done.14), channel_id=1, source_target_pairs={{2,0},{3,1},{4,2},{5,3},{6,4},{7,5},{10,8},{11,9},{12,10},{13,11},... | collective-permute-start | bytes 1572872 | tf_op jit(solution)/shard_map/ppermute | solution.py:137
  138.8 48.1 %collective-permute-start.11 = (f32[8,128,128]{2,1,0:T(8,128)}, f32[8,128,128]{2,1,0:T(8,128)}, u32[]{:S(2)}, u32[]{:S(2)}) collective-permute-start(f32[8,128,128]{2,1,0:T(8,128)} %collective-permute-done.10), channel_id=1, source_target_pairs={{2,0},{3,1},{4,2},{5,3},{6,4},{7,5},{10,8},{11,9},{12,10},{13,11},... | collective-permute-start | bytes 1572872 | tf_op jit(solution)/shard_map/ppermute | solution.py:137
  185.1 4.3 %copy-start.4 = (bf16[1,768,2048]{2,1,0:T(8,128)(2,1)S(1)}, bf16[1,768,2048]{2,1,0:T(8,128)(2,1)}, u32[]{:S(2)}) copy-start(bf16[1,768,2048]{2,1,0:T(8,128)(2,1)} %k_ref.7) | copy-start | bytes 9437188
  185.1 4.3 %copy-start.7 = (bf16[1,768,2048]{2,1,0:T(8,128)(2,1)S(1)}, bf16[1,768,2048]{2,1,0:T(8,128)(2,1)}, u32[]{:S(2)}) copy-start(bf16[1,768,2048]{2,1,0:T(8,128)(2,1)} %v_ref.7) | copy-start | bytes 9437188
  185.1 4.3 %copy-start.10 = (f32[16,128,128]{2,1,0:T(8,128)S(1)}, f32[16,128,128]{2,1,0:T(8,128)}, u32[]{:S(2)}) copy-start(f32[16,128,128]{2,1,0:T(8,128)} %pad_maximum_fusion.prior_ref) | copy-start | bytes 3145732

commit v2 on v1

--- a/solution.py
+++ b/solution.py
@@ -87,7 +87,7 @@
     )
 
 
-PARAMS = pltpu.CompilerParams(vmem_limit_bytes=40 * 1024 * 1024)
+PARAMS = pltpu.CompilerParams(vmem_limit_bytes=60 * 1024 * 1024)
 
 
 def on_device(queries, keys, values, grad_out, node_ids, flags, gain):
@@ -163,7 +163,7 @@
         jnp.sum(prior * qg, axis=(1, 2)) for prior, (_, qg) in zip(priors, states)
     ])
     term = scale * (jnp.sum(near, axis=(1, 2)) + far)
-    total = lax.psum(term, ("dp", "ctx"))
+    total = jnp.sum(lax.all_gather(term, ("dp", "ctx")), axis=0)
 
     wide_out = jax.ShapeDtypeStruct(queries.shape, jnp.bfloat16)
     grads = pl.pallas_call(

time: 217 us -> 244 us (1.12)
  blocking collectives: 42.2 us -> 75.3 us
  local copies, waits for them, and re-layouts: 13.3 us -> 0.04 us
  Pallas kernels: 41 us -> 47.7 us
    all_gather x0 -> x1, blocking collectives: none -> 75.3 us  [on_device(): total = jnp.sum(lax.all_gather(term, ('dp', 'ctx')), axis=0)]
    psum x1 -> x0, blocking collectives: 42.2 us -> none  [on_device(): total = lax.psum(term, ('dp', 'ctx'))]
    unnamed x36 -> x18, local copies, waits for them, and re-layouts: 13.3 us -> 0.04 us
    pallas_call x2, Pallas kernels: 5.88 us -> 9.99 us  [on_device(): pl.pallas_call(state_kernel, grid=(group // PER,), in_specs=[wide(c * gro...]
    ppermute x6, waiting for transfers between devices: 31.1 us -> 28.3 us  [on_device(): kv_move = lax.ppermute(kv_move, 'ctx', up)]
    ppermute x6, waiting for transfers between devices: 18.7 us -> 21.4 us  [on_device(): qg_move = lax.ppermute(qg_move, 'ctx', down)]
    pallas_call x1, Pallas kernels: 8.11 us -> 10.7 us  [on_device(): pl.pallas_call(term_kernel, grid=(H // PER,), in_specs=[wide(0)] * 4 + [s...]
  transfers between devices with their start and end apart: 16 -> 16, of which waited for: 10 -> 10; matrix products, arithmetic and copies ran while one was open for 5% -> 5% of each run, Pallas kernels for 5% -> 6%
where the time goes in v2:
time: 244 us; the launch traced here: 243 us
  blocking collectives  75.3 us (31%)
  waiting for transfers between devices  63.9 us (26%)
  Pallas kernels  47.7 us (20%)
  starting transfers between devices  41.7 us (17%)
  other arithmetic  13.7 us (6%)
    all_gather x1, blocking collectives, on_device(): total = jnp.sum(lax.all_gather(term, ('dp', 'ctx')), axis=0)  75.3 us
    ppermute x6, waiting for transfers between devices, on_device(): kv_move = lax.ppermute(kv_move, 'ctx', up)  28.3 us
    ppermute x6, starting transfers between devices, on_device(): kv_move = lax.ppermute(kv_move, 'ctx', up)  27.8 us
    pallas_call x1, Pallas kernels, on_device(): pl.pallas_call(grad_kernel, grid=(H // PER,), in_specs=[wide(0)] * 4 + [s...  26.9 us
    ppermute x6, waiting for transfers between devices, on_device(): qg_move = lax.ppermute(qg_move, 'ctx', down)  21.4 us
    ppermute x2, waiting for transfers between devices, on_device(): kv_other = lax.ppermute(kv, 'ctx', swap)  14.2 us
    pallas_call x1, Pallas kernels, on_device(): pl.pallas_call(term_kernel, grid=(H // PER,), in_specs=[wide(0)] * 4 + [s...  10.7 us
    pallas_call x2, Pallas kernels, on_device(): pl.pallas_call(state_kernel, grid=(group // PER,), in_specs=[wide(c * gro...  9.99 us
  transfers between devices with their start and end apart: 16, of which 10 were waited for; matrix products, arithmetic and copies ran while one was open for 5% of the time, Pallas kernels for 6%

profile of v2, /device:TPU:0, one launch (start us, length us, event | category | flops | bytes accessed | tf_op | source)
XLA Modules:
  0.0 243.1 jit_solution(3964146300756600953)
XLA Ops:
  0.6 5.0 %states.3 = (f32[8,128,128]{2,1,0:T(8,128)}, f32[8,128,128]{2,1,0:T(8,128)}) custom-call(bf16[1,768,2048]{2,1,0:T(8,128)(2,1)} %q_ref.7, bf16[1,768,2048]{2,1,0:T(8,128)(2,1)} %k_ref.7, bf16[1,768,2048]{2,1,0:T(8,128)(2,1)} %v_ref.7, bf16[1,768,2048]{2,1,0:T(8,128)(2,1)} %g_ref.7), custom_call_target="tpu_custom_call" | custom-call | flops 402653184 | bytes 7340032 | tf_op jit(solution)/shard_map/states/pallas_call | solution.py:108
  5.6 3.0 %collective-permute-start.4 = (f32[8,128,128]{2,1,0:T(8,128)}, f32[8,128,128]{2,1,0:T(8,128)S(1)}, u32[]{:S(2)}, u32[]{:S(2)}) collective-permute-start(f32[8,128,128]{2,1,0:T(8,128)} %get-tuple-element.12), channel_id=1, source_target_pairs={{0,1},{1,0},{2,3},{3,2},{4,5},{5,4},{6,7},{7,6},{8,9},{9,8},{10,11... | collective-permute-start | bytes 1572872 | tf_op jit(solution)/shard_map/ppermute | solution.py:127
  8.6 5.0 %states.2 = (f32[8,128,128]{2,1,0:T(8,128)}, f32[8,128,128]{2,1,0:T(8,128)}) custom-call(bf16[1,768,2048]{2,1,0:T(8,128)(2,1)} %q_ref.7, bf16[1,768,2048]{2,1,0:T(8,128)(2,1)} %k_ref.7, bf16[1,768,2048]{2,1,0:T(8,128)(2,1)} %v_ref.7, bf16[1,768,2048]{2,1,0:T(8,128)(2,1)} %g_ref.7), custom_call_target="tpu_custom_call" | custom-call | flops 402653184 | bytes 7340032 | tf_op jit(solution)/shard_map/states/pallas_call | solution.py:108
  13.6 0.1 collective-permute-start
  13.8 7.9 %collective-permute-done.4 = f32[8,128,128]{2,1,0:T(8,128)S(1)} collective-permute-done((f32[8,128,128]{2,1,0:T(8,128)}, f32[8,128,128]{2,1,0:T(8,128)S(1)}, u32[]{:S(2)}, u32[]{:S(2)}) %collective-permute-start.4) | collective-permute-done | bytes 524320 | tf_op jit(solution)/shard_map/ppermute | solution.py:127
  21.6 0.1 add.67
  21.7 4.0 %collective-permute-start.5 = (f32[8,128,128]{2,1,0:T(8,128)S(1)}, f32[8,128,128]{2,1,0:T(8,128)S(1)}, u32[]{:S(2)}, u32[]{:S(2)}) collective-permute-start(f32[8,128,128]{2,1,0:T(8,128)S(1)} %add.67), channel_id=1, source_target_pairs={{0,2},{1,3},{2,4},{3,5},{4,6},{5,7},{8,10},{9,11},{10,12},{11,13},... | collective-permute-start | bytes 1572872 | tf_op jit(solution)/shard_map/ppermute | solution.py:136
  25.7 6.3 %collective-permute-done = f32[8,128,128]{2,1,0:T(8,128)S(1)} collective-permute-done((f32[8,128,128]{2,1,0:T(8,128)}, f32[8,128,128]{2,1,0:T(8,128)S(1)}, u32[]{:S(2)}, u32[]{:S(2)}) %collective-permute-start) | collective-permute-done | bytes 524320 | tf_op jit(solution)/shard_map/ppermute | solution.py:127
  32.0 1.1 add.63
  33.1 3.7 %collective-permute-start.1 = (f32[8,128,128]{2,1,0:T(8,128)S(1)}, f32[8,128,128]{2,1,0:T(8,128)S(1)}, u32[]{:S(2)}, u32[]{:S(2)}) collective-permute-start(f32[8,128,128]{2,1,0:T(8,128)S(1)} %add.63), channel_id=1, source_target_pairs={{0,2},{1,3},{2,4},{3,5},{4,6},{5,7},{8,10},{9,11},{10,12},{11,13},... | collective-permute-start | bytes 1572872 | tf_op jit(solution)/shard_map/ppermute | solution.py:136
  36.9 0.0 collective-permute-done.5
  36.9 0.0 copy-start.4
  36.9 4.3 %collective-permute-start.6 = (f32[8,128,128]{2,1,0:T(8,128)S(1)}, f32[8,128,128]{2,1,0:T(8,128)}, u32[]{:S(2)}, u32[]{:S(2)}) collective-permute-start(f32[8,128,128]{2,1,0:T(8,128)S(1)} %collective-permute-done.5), channel_id=1, source_target_pairs={{0,2},{1,3},{2,4},{3,5},{4,6},{5,7},{8,10},{9,11},{10,12},{11,13},... | collective-permute-start | bytes 1572872 | tf_op jit(solution)/shard_map/ppermute | solution.py:136
  41.1 8.0 %collective-permute-done.1 = f32[8,128,128]{2,1,0:T(8,128)S(1)} collective-permute-done((f32[8,128,128]{2,1,0:T(8,128)S(1)}, f32[8,128,128]{2,1,0:T(8,128)S(1)}, u32[]{:S(2)}, u32[]{:S(2)}) %collective-permute-start.1) | collective-permute-done | bytes 524320 | tf_op jit(solution)/shard_map/ppermute | solution.py:136
  49.2 5.2 %collective-permute-start.2 = (f32[8,128,128]{2,1,0:T(8,128)S(1)}, f32[8,128,128]{2,1,0:T(8,128)}, u32[]{:S(2)}, u32[]{:S(2)}) collective-permute-start(f32[8,128,128]{2,1,0:T(8,128)S(1)} %collective-permute-done.1), channel_id=1, source_target_pairs={{0,2},{1,3},{2,4},{3,5},{4,6},{5,7},{8,10},{9,11},{10,12},{11,13},... | collective-permute-start | bytes 1572872 | tf_op jit(solution)/shard_map/ppermute | solution.py:136
  54.4 1.5 collective-permute-start.12
  55.9 4.6 %collective-permute-done.6 = f32[8,128,128]{2,1,0:T(8,128)} collective-permute-done((f32[8,128,128]{2,1,0:T(8,128)S(1)}, f32[8,128,128]{2,1,0:T(8,128)}, u32[]{:S(2)}, u32[]{:S(2)}) %collective-permute-start.6) | collective-permute-done | bytes 524320 | tf_op jit(solution)/shard_map/ppermute | solution.py:136
  60.4 5.3 %collective-permute-start.7 = (f32[8,128,128]{2,1,0:T(8,128)}, f32[8,128,128]{2,1,0:T(8,128)}, u32[]{:S(2)}, u32[]{:S(2)}) collective-permute-start(f32[8,128,128]{2,1,0:T(8,128)} %collective-permute-done.6), channel_id=1, source_target_pairs={{0,2},{1,3},{2,4},{3,5},{4,6},{5,7},{8,10},{9,11},{10,12},{11,13},... | collective-permute-start | bytes 1572872 | tf_op jit(solution)/shard_map/ppermute | solution.py:136
  65.7 1.5 collective-permute-start.8
  67.2 4.4 %collective-permute-done.2 = f32[8,128,128]{2,1,0:T(8,128)} collective-permute-done((f32[8,128,128]{2,1,0:T(8,128)S(1)}, f32[8,128,128]{2,1,0:T(8,128)}, u32[]{:S(2)}, u32[]{:S(2)}) %collective-permute-start.2) | collective-permute-done | bytes 524320 | tf_op jit(solution)/shard_map/ppermute | solution.py:136
  71.7 5.3 %collective-permute-start.3 = (f32[8,128,128]{2,1,0:T(8,128)}, f32[8,128,128]{2,1,0:T(8,128)}, u32[]{:S(2)}, u32[]{:S(2)}) collective-permute-start(f32[8,128,128]{2,1,0:T(8,128)} %collective-permute-done.2), channel_id=1, source_target_pairs={{0,2},{1,3},{2,4},{3,5},{4,6},{5,7},{8,10},{9,11},{10,12},{11,13},... | collective-permute-start | bytes 1572872 | tf_op jit(solution)/shard_map/ppermute | solution.py:136
  77.0 0.0 collective-permute-done.12
  77.0 6.0 %collective-permute-done.7 = f32[8,128,128]{2,1,0:T(8,128)} collective-permute-done((f32[8,128,128]{2,1,0:T(8,128)}, f32[8,128,128]{2,1,0:T(8,128)}, u32[]{:S(2)}, u32[]{:S(2)}) %collective-permute-start.7) | collective-permute-done | bytes 524320 | tf_op jit(solution)/shard_map/ppermute | solution.py:136
  83.0 2.5 %multiply_reduce_fusion = (f32[8]{0:T(128)S(1)}, f32[8,128,128]{2,1,0:T(8,128)S(1)}, f32[8,128,128]{2,1,0:T(8,128)}) fusion(f32[8,128,128]{2,1,0:T(8,128)} %get-tuple-element.14, f32[8,128,128]{2,1,0:T(8,128)} %collective-permute-done.7, f32[8,128,128]{2,1,0:T(8,128)} %collective-permute-done.6, f32[8,128,128]{2,1,0:T(8,128)} %copy-done.4, ...), kind=kLoop, calls=%fused_computation.2 | loop fusion | flops 917496 | bytes 4194337 | tf_op jit(solution)/shard_map/reduce_sum | solution.py:163
  85.5 1.4 collective-permute-start.13
  86.9 5.3 %collective-permute-done.3 = f32[8,128,128]{2,1,0:T(8,128)} collective-permute-done((f32[8,128,128]{2,1,0:T(8,128)}, f32[8,128,128]{2,1,0:T(8,128)}, u32[]{:S(2)}, u32[]{:S(2)}) %collective-permute-start.3) | collective-permute-done | bytes 524320 | tf_op jit(solution)/shard_map/ppermute | solution.py:136
  92.2 2.2 multiply_reduce_fusion.1
  94.4 1.3 collective-permute-start.9
  95.7 0.9 and_convert_fusion.seen_ref
  96.7 2.0 collective-permute-done.13
  98.7 1.3 collective-permute-start.14
  100.0 11.8 %collective-permute-done.9 = f32[8,128,128]{2,1,0:T(8,128)S(1)} collective-permute-done((f32[8,128,128]{2,1,0:T(8,128)}, f32[8,128,128]{2,1,0:T(8,128)S(1)}, u32[]{:S(2)}, u32[]{:S(2)}) %collective-permute-start.9) | collective-permute-done | bytes 524320 | tf_op jit(solution)/shard_map/ppermute | solution.py:137
  111.8 1.3 collective-permute-start.10
  113.1 10.7 %gain_term.1 = f32[16,1,128]{2,1,0:T(1,128)} custom-call(bf16[1,768,2048]{2,1,0:T(8,128)(2,1)} %q_ref.7, bf16[1,768,2048]{2,1,0:T(8,128)(2,1)} %k_ref.7, bf16[1,768,2048]{2,1,0:T(8,128)(2,1)} %v_ref.7, bf16[1,768,2048]{2,1,0:T(8,128)(2,1)} %g_ref.7, f32[6,128,128]{2,1,0:T(8,128)} %and_convert_fusion.seen_ref), custom_call_target="tpu_custom_call" | custom-call | flops 3221225472 | bytes 12582912 | tf_op jit(solution)/shard_map/gain_term/pallas_call | solution.py:151
  123.8 0.9 reduce_sum.38
  124.7 0.6 broadcast_multiply_fusion.1.factor_ref
  125.3 1.3 collective-permute-start.15
  126.6 0.1 fusion.1
  126.7 7.6 %collective-permute-done.10 = f32[8,128,128]{2,1,0:T(8,128)S(1)} collective-permute-done((f32[8,128,128]{2,1,0:T(8,128)S(1)}, f32[8,128,128]{2,1,0:T(8,128)S(1)}, u32[]{:S(2)}, u32[]{:S(2)}) %collective-permute-start.10) | collective-permute-done | bytes 524320 | tf_op jit(solution)/shard_map/ppermute | solution.py:137
  134.3 1.3 collective-permute-start.11
  135.6 1.0 pad_maximum_fusion.prior_ref
  136.6 75.3 %all-gather = f32[32,1,16]{2,1,0:T(1,128)S(1)} all-gather(f32[1,1,16]{2,1,0:T(1,128)S(1)} %fusion.1), channel_id=1, replica_groups=mesh['dp'=4,'ctx'=8] {'dp','ctx'}, dimensions={0}, use_global_device_ids=true | all-gather | bytes 2112 | tf_op jit(solution)/shard_map/all_gather | solution.py:166
  211.9 0.1 reduce_sum.42
  211.9 0.5 broadcast_multiply_fusion
  212.4 1.5 add_add_fusion
  213.9 1.2 add_add_fusion.1
  215.1 1.1 pad_maximum_fusion.1.later_ref
  216.2 26.9 %grads.1 = (bf16[1,768,2048]{2,1,0:T(8,128)(2,1)}, bf16[1,768,2048]{2,1,0:T(8,128)(2,1)}, bf16[1,768,2048]{2,1,0:T(8,128)(2,1)}) custom-call(bf16[1,768,2048]{2,1,0:T(8,128)(2,1)} %q_ref.7, bf16[1,768,2048]{2,1,0:T(8,128)(2,1)} %k_ref.7, bf16[1,768,2048]{2,1,0:T(8,128)(2,1)} %v_ref.7, bf16[1,768,2048]{2,1,0:T(8,128)(2,1)} %g_ref.7, ...), custom_call_target="tpu_custom_call" | custom-call | flops 8053063680 | bytes 22020096 | tf_op jit(solution)/shard_map/grads/pallas_call | solution.py:169
  (24 shorter events, 0.1 us)
Async XLA Ops:
  5.6 16.0 %copy-start.5 = (f32[8,128,128]{2,1,0:T(8,128)S(1)}, f32[8,128,128]{2,1,0:T(8,128)}, u32[]{:S(2)}) copy-start(f32[8,128,128]{2,1,0:T(8,128)} %get-tuple-element.12) | copy-start | bytes 1572868
  5.6 16.0 %collective-permute-start.4 = (f32[8,128,128]{2,1,0:T(8,128)}, f32[8,128,128]{2,1,0:T(8,128)S(1)}, u32[]{:S(2)}, u32[]{:S(2)}) collective-permute-start(f32[8,128,128]{2,1,0:T(8,128)} %get-tuple-element.12), channel_id=1, source_target_pairs={{0,1},{1,0},{2,3},{3,2},{4,5},{5,4},{6,7},{7,6},{8,9},{9,8},{10,11... | collective-permute-start | bytes 1572872 | tf_op jit(solution)/shard_map/ppermute | solution.py:127
  13.6 40.8 %copy-start.1 = (f32[8,128,128]{2,1,0:T(8,128)S(1)}, f32[8,128,128]{2,1,0:T(8,128)}, u32[]{:S(2)}) copy-start(f32[8,128,128]{2,1,0:T(8,128)} %get-tuple-element.14) | copy-start | bytes 1572868
  13.6 52.1 %copy-start = (f32[8,128,128]{2,1,0:T(8,128)S(1)}, f32[8,128,128]{2,1,0:T(8,128)}, u32[]{:S(2)}) copy-start(f32[8,128,128]{2,1,0:T(8,128)} %get-tuple-element.13) | copy-start | bytes 1572868
  13.6 18.4 %collective-permute-start = (f32[8,128,128]{2,1,0:T(8,128)}, f32[8,128,128]{2,1,0:T(8,128)S(1)}, u32[]{:S(2)}, u32[]{:S(2)}) collective-permute-start(f32[8,128,128]{2,1,0:T(8,128)} %get-tuple-element.11), channel_id=1, source_target_pairs={{0,1},{1,0},{2,3},{3,2},{4,5},{5,4},{6,7},{7,6},{8,9},{9,8},{10,11... | collective-permute-start | bytes 1572872 | tf_op jit(solution)/shard_map/ppermute | solution.py:127
  21.7 15.2 %collective-permute-start.5 = (f32[8,128,128]{2,1,0:T(8,128)S(1)}, f32[8,128,128]{2,1,0:T(8,128)S(1)}, u32[]{:S(2)}, u32[]{:S(2)}) collective-permute-start(f32[8,128,128]{2,1,0:T(8,128)S(1)} %add.67), channel_id=1, source_target_pairs={{0,2},{1,3},{2,4},{3,5},{4,6},{5,7},{8,10},{9,11},{10,12},{11,13},... | collective-permute-start | bytes 1572872 | tf_op jit(solution)/shard_map/ppermute | solution.py:136
  33.1 16.1 %collective-permute-start.1 = (f32[8,128,128]{2,1,0:T(8,128)S(1)}, f32[8,128,128]{2,1,0:T(8,128)S(1)}, u32[]{:S(2)}, u32[]{:S(2)}) collective-permute-start(f32[8,128,128]{2,1,0:T(8,128)S(1)} %add.63), channel_id=1, source_target_pairs={{0,2},{1,3},{2,4},{3,5},{4,6},{5,7},{8,10},{9,11},{10,12},{11,13},... | collective-permute-start | bytes 1572872 | tf_op jit(solution)/shard_map/ppermute | solution.py:136
  36.9 28.9 %copy-start.4 = (f32[8,128,128]{2,1,0:T(8,128)}, f32[8,128,128]{2,1,0:T(8,128)S(1)}, u32[]{:S(2)}) copy-start(f32[8,128,128]{2,1,0:T(8,128)S(1)} %collective-permute-done.5) | copy-start | bytes 1572868
  36.9 23.5 %collective-permute-start.6 = (f32[8,128,128]{2,1,0:T(8,128)S(1)}, f32[8,128,128]{2,1,0:T(8,128)}, u32[]{:S(2)}, u32[]{:S(2)}) collective-permute-start(f32[8,128,128]{2,1,0:T(8,128)S(1)} %collective-permute-done.5), channel_id=1, source_target_pairs={{0,2},{1,3},{2,4},{3,5},{4,6},{5,7},{8,10},{9,11},{10,12},{11,13},... | collective-permute-start | bytes 1572872 | tf_op jit(solution)/shard_map/ppermute | solution.py:136
  49.2 16.5 %copy-start.2 = (f32[8,128,128]{2,1,0:T(8,128)}, f32[8,128,128]{2,1,0:T(8,128)S(1)}, u32[]{:S(2)}) copy-start(f32[8,128,128]{2,1,0:T(8,128)S(1)} %collective-permute-done.1) | copy-start | bytes 1572868
  49.2 22.5 %collective-permute-start.2 = (f32[8,128,128]{2,1,0:T(8,128)S(1)}, f32[8,128,128]{2,1,0:T(8,128)}, u32[]{:S(2)}, u32[]{:S(2)}) collective-permute-start(f32[8,128,128]{2,1,0:T(8,128)S(1)} %collective-permute-done.1), channel_id=1, source_target_pairs={{0,2},{1,3},{2,4},{3,5},{4,6},{5,7},{8,10},{9,11},{10,12},{11,13},... | collective-permute-start | bytes 1572872 | tf_op jit(solution)/shard_map/ppermute | solution.py:136
  54.4 22.6 %collective-permute-start.12 = (f32[8,128,128]{2,1,0:T(8,128)S(1)}, f32[8,128,128]{2,1,0:T(8,128)S(1)}, u32[]{:S(2)}, u32[]{:S(2)}) collective-permute-start(f32[8,128,128]{2,1,0:T(8,128)S(1)} %copy-done.1), channel_id=1, source_target_pairs={{0,1},{1,0},{2,3},{3,2},{4,5},{5,4},{6,7},{7,6},{8,9},{9,8},{10,11... | collective-permute-start | bytes 1572872 | tf_op jit(solution)/shard_map/ppermute | solution.py:128
  60.4 22.6 %collective-permute-start.7 = (f32[8,128,128]{2,1,0:T(8,128)}, f32[8,128,128]{2,1,0:T(8,128)}, u32[]{:S(2)}, u32[]{:S(2)}) collective-permute-start(f32[8,128,128]{2,1,0:T(8,128)} %collective-permute-done.6), channel_id=1, source_target_pairs={{0,2},{1,3},{2,4},{3,5},{4,6},{5,7},{8,10},{9,11},{10,12},{11,13},... | collective-permute-start | bytes 1572872 | tf_op jit(solution)/shard_map/ppermute | solution.py:136
  65.7 21.2 %collective-permute-start.8 = (f32[8,128,128]{2,1,0:T(8,128)S(1)}, f32[8,128,128]{2,1,0:T(8,128)S(1)}, u32[]{:S(2)}, u32[]{:S(2)}) collective-permute-start(f32[8,128,128]{2,1,0:T(8,128)S(1)} %copy-done), channel_id=1, source_target_pairs={{0,1},{1,0},{2,3},{3,2},{4,5},{5,4},{6,7},{7,6},{8,9},{9,8},{10,11... | collective-permute-start | bytes 1572872 | tf_op jit(solution)/shard_map/ppermute | solution.py:128
  71.7 20.5 %collective-permute-start.3 = (f32[8,128,128]{2,1,0:T(8,128)}, f32[8,128,128]{2,1,0:T(8,128)}, u32[]{:S(2)}, u32[]{:S(2)}) collective-permute-start(f32[8,128,128]{2,1,0:T(8,128)} %collective-permute-done.2), channel_id=1, source_target_pairs={{0,2},{1,3},{2,4},{3,5},{4,6},{5,7},{8,10},{9,11},{10,12},{11,13},... | collective-permute-start | bytes 1572872 | tf_op jit(solution)/shard_map/ppermute | solution.py:136
  77.0 15.2 %copy-start.3 = (f32[8,128,128]{2,1,0:T(8,128)S(1)}, f32[8,128,128]{2,1,0:T(8,128)}, u32[]{:S(2)}) copy-start(f32[8,128,128]{2,1,0:T(8,128)} %copy-done.2) | copy-start | bytes 1572868
  85.5 10.2 %copy-start.7 = (s32[1,768]{1,0:T(1,128)S(1)}, s32[1,768]{1,0:T(1,128)}, u32[]{:S(2)}) copy-start(s32[1,768]{1,0:T(1,128)} %param.11) | copy-start | bytes 9220
  85.5 10.2 %copy-start.6 = (s32[1,768]{1,0:T(1,128)S(1)}, s32[1,768]{1,0:T(1,128)}, u32[]{:S(2)}) copy-start(s32[1,768]{1,0:T(1,128)} %param.12) | copy-start | bytes 9220
  85.5 13.2 %collective-permute-start.13 = (f32[8,128,128]{2,1,0:T(8,128)}, f32[8,128,128]{2,1,0:T(8,128)}, u32[]{:S(2)}, u32[]{:S(2)}) collective-permute-start(f32[8,128,128]{2,1,0:T(8,128)} %get-tuple-element.23), channel_id=1, source_target_pairs={{2,0},{3,1},{4,2},{5,3},{6,4},{7,5},{10,8},{11,9},{12,10},{13,11},... | collective-permute-start | bytes 1572872 | tf_op jit(solution)/shard_map/ppermute | solution.py:137
  94.4 17.4 %collective-permute-start.9 = (f32[8,128,128]{2,1,0:T(8,128)}, f32[8,128,128]{2,1,0:T(8,128)S(1)}, u32[]{:S(2)}, u32[]{:S(2)}) collective-permute-start(f32[8,128,128]{2,1,0:T(8,128)} %get-tuple-element.22), channel_id=1, source_target_pairs={{2,0},{3,1},{4,2},{5,3},{6,4},{7,5},{10,8},{11,9},{12,10},{13,11},... | collective-permute-start | bytes 1572872 | tf_op jit(solution)/shard_map/ppermute | solution.py:137
  96.7 28.1 %copy-start.8 = (f32[16]{0:T(128)S(1)}, f32[16]{0:T(128)}, u32[]{:S(2)}) copy-start(f32[16]{0:T(128)} %param.13) | copy-start | bytes 196
  98.7 26.6 %collective-permute-start.14 = (f32[8,128,128]{2,1,0:T(8,128)}, f32[8,128,128]{2,1,0:T(8,128)}, u32[]{:S(2)}, u32[]{:S(2)}) collective-permute-start(f32[8,128,128]{2,1,0:T(8,128)} %collective-permute-done.13), channel_id=1, source_target_pairs={{2,0},{3,1},{4,2},{5,3},{6,4},{7,5},{10,8},{11,9},{12,10},{13,11},... | collective-permute-start | bytes 1572872 | tf_op jit(solution)/shard_map/ppermute | solution.py:137
  111.8 22.5 %collective-permute-start.10 = (f32[8,128,128]{2,1,0:T(8,128)S(1)}, f32[8,128,128]{2,1,0:T(8,128)S(1)}, u32[]{:S(2)}, u32[]{:S(2)}) collective-permute-start(f32[8,128,128]{2,1,0:T(8,128)S(1)} %collective-permute-done.9), channel_id=1, source_target_pairs={{2,0},{3,1},{4,2},{5,3},{6,4},{7,5},{10,8},{11,9},{12,10},{13,11},... | collective-permute-start | bytes 1572872 | tf_op jit(solution)/shard_map/ppermute | solution.py:137
  125.3 87.1 %collective-permute-start.15 = (f32[8,128,128]{2,1,0:T(8,128)}, f32[8,128,128]{2,1,0:T(8,128)}, u32[]{:S(2)}, u32[]{:S(2)}) collective-permute-start(f32[8,128,128]{2,1,0:T(8,128)} %collective-permute-done.14), channel_id=1, source_target_pairs={{2,0},{3,1},{4,2},{5,3},{6,4},{7,5},{10,8},{11,9},{12,10},{13,11},... | collective-permute-start | bytes 1572872 | tf_op jit(solution)/shard_map/ppermute | solution.py:137
  134.3 79.6 %collective-permute-start.11 = (f32[8,128,128]{2,1,0:T(8,128)S(1)}, f32[8,128,128]{2,1,0:T(8,128)}, u32[]{:S(2)}, u32[]{:S(2)}) collective-permute-start(f32[8,128,128]{2,1,0:T(8,128)S(1)} %collective-permute-done.10), channel_id=1, source_target_pairs={{2,0},{3,1},{4,2},{5,3},{6,4},{7,5},{10,8},{11,9},{12,10},{13,11},... | collective-permute-start | bytes 1572872 | tf_op jit(solution)/shard_map/ppermute | solution.py:137
